TPU v7x, 128 devices: a whole 4x4x4 slice. The times are simulated.
128 devices in a mesh: lon: 8 (over z_lo, x), lat: 16 (over y, z_hi, core).
Axes of the slice: x: 4, y: 4, z: 4 (z_hi: 2, z_lo: 2; z = z_hi * 2 + z_lo), core: 2. Of those that a mesh axis runs over, the one named last changes fastest.
Arguments:
- tracers: float32 [2, 16, 256, 2048], P(None, None, 'lat', 'lon'), may hold values from -6 to 6
- east_velocity: float32 [16, 256, 2048], P(None, 'lat', 'lon'), may hold values from -0.3 to 0.3
- north_velocity: float32 [16, 256, 2048], P(None, 'lat', 'lon'), may hold values from -0.3 to 0.3
- ocean_levels: int32 [256, 2048], P('lat', 'lon'), may hold values from 0 to 16
- fold_partner: int32 [2048], P('lon'), may hold values from 0 to 2047, as said below
- atm_flux: float32 [2, 65536], P(None, ('lon', 'lat')), may hold values from -6 to 6
- remap_index: int32 [4, 256, 2048], P(None, 'lat', 'lon'), may hold values from 0 to 65535
- remap_weight: float32 [4, 256, 2048], P(None, 'lat', 'lon'), may hold values from 0 to 0.5
Outputs:
- tracers_out: float32 [2, 16, 256, 2048], P(None, None, 'lat', 'lon')
Inputs may be any that keep to these rules, and one draw needn't show every extreme that they name: `fold_partner`: the partners of the columns of longitude tile t (global column i lies in tile i // 256) lie among the 512 columns of tiles (7 - t) mod 8 and (8 - t) mod 8; both of these tiles hold partners of tile t.
All inputs are finite; a program needn't handle non-finite values.
Results may differ from a plain program's by a relative error of at most 0.0003.
Values sent between devices are 32-bit elements; how exact they have to be, the bound alone decides.
No kernel may reach another device: no remote copies, remote signals or barrier semaphores. Data moves between devices by JAX's collectives and lax.ppermute only.
A program may use at most 128 MiB of HBM per device.

v0:
```python
import jax
import jax.numpy as jnp
from jax import lax
from jax.sharding import PartitionSpec as P

STEPS = 3


def extended_2(cells, sides, width, closed):
    for axis, dim in sides:
        count = lax.axis_size(axis)
        ends = count if closed else count - 1
        head = lax.slice_in_dim(cells, 0, width, axis=dim)
        tail = lax.slice_in_dim(cells, cells.shape[dim] - width, cells.shape[dim], axis=dim)
        cells = jnp.concatenate(
            [
                lax.ppermute(tail, axis, [(i, (i + 1) % count) for i in range(ends)]),
                cells,
                lax.ppermute(head, axis, [((i + 1) % count, i) for i in range(ends)]),
            ],
            axis=dim,
        )
    return cells


def laplace(values_in, east_mask, north_mask):
    east_flux = east_mask * (values_in[..., 1:] - values_in[..., :-1])
    north_flux = north_mask * (values_in[..., 1:, :] - values_in[..., :-1, :])
    return (
        east_flux[..., 1:-1, 1:]
        - east_flux[..., 1:-1, :-1]
        + (north_flux[..., 1:, 1:-1] - north_flux[..., :-1, 1:-1])
    )


def advance(extended, wet_mask, east_ext, north_ext, surface):
    east_mask = wet_mask[..., :-1] * wet_mask[..., 1:]
    north_mask = wet_mask[:, :-1, :] * wet_mask[:, 1:, :]
    lap_once = laplace(extended, east_mask, north_mask)
    inner_east = east_mask[:, 1:-1, 1:-1]
    inner_north = north_mask[:, 1:-1, 1:-1]
    lap_twice = laplace(lap_once, inner_east, inner_north)
    near_cells = extended[..., 1:-1, 1:-1]
    east_flux = (
        east_ext[:, 1:-1, 1:-2] * inner_east * 0.5 * (near_cells[..., :-1] + near_cells[..., 1:])
    )
    north_flux = (
        north_ext[:, 1:-2, 1:-1]
        * inner_north
        * 0.5
        * (near_cells[..., :-1, :] + near_cells[..., 1:, :])
    )
    spread = (
        east_flux[..., 1:-1, 1:]
        - east_flux[..., 1:-1, :-1]
        + (north_flux[..., 1:, 1:-1] - north_flux[..., :-1, 1:-1])
    )
    centre_cells = extended[..., 2:-2, 2:-2]
    wet_cells = wet_mask[:, 2:-2, 2:-2]
    vert_mask = wet_cells[:-1] * wet_cells[1:]
    vert_flux = vert_mask * (centre_cells[:, 1:] - centre_cells[:, :-1])
    zero_level = jnp.zeros_like(centre_cells[:, :1])
    vertical = jnp.concatenate([vert_flux, zero_level], axis=1) - jnp.concatenate(
        [zero_level, vert_flux], axis=1
    )
    forcing = jnp.concatenate([surface[:, None], jnp.zeros_like(centre_cells[:, 1:])], axis=1)
    tendency = (
        -spread
        + 0.08 * lap_once[..., 1:-1, 1:-1]
        - 0.01 * lap_twice
        + 0.1 * vertical
        + 0.5 * forcing
    )
    return centre_cells + wet_cells * tendency


def per_device(
    tracers,
    east_velocity,
    north_velocity,
    ocean_levels,
    fold_partner,
    atm_flux,
    remap_index,
    remap_weight,
):
    levels = tracers.shape[1]
    cols_dev = tracers.shape[3]
    lat_place = lax.axis_index("lat")
    is_top = lat_place == lax.axis_size("lat") - 1
    keep_top = jnp.where(is_top, 0.0, 1.0).astype(jnp.float32)
    north_fixed = north_velocity.at[:, -1, :].multiply(keep_top)
    statics = jnp.concatenate(
        [east_velocity, north_fixed, ocean_levels.astype(jnp.float32)[None]], axis=0
    )
    statics = extended_2(statics, (("lat", 1),), 2, False)
    static_ghost = jnp.concatenate(
        [
            jnp.zeros((2 * levels, 2, cols_dev), jnp.float32),
            jnp.full((1, 2, cols_dev), float(levels), jnp.float32),
        ],
        axis=0,
    )
    static_top = jnp.where(is_top, static_ghost, statics[:, -2:])
    statics = jnp.concatenate([statics[:, :-2], static_top], axis=1)
    statics = extended_2(statics, (("lon", 2),), 2, True)
    east_ext = statics[:levels]
    north_ext = statics[levels : 2 * levels]
    depth_ext = statics[2 * levels]
    level_index = jnp.arange(levels).astype(jnp.float32)
    wet_mask = (level_index[:, None, None] < depth_ext[None]).astype(jnp.float32)
    gathered = lax.all_gather(atm_flux, ("lon", "lat"), axis=1, tiled=True)
    surface = jnp.sum(remap_weight[None] * jnp.take(gathered, remap_index, axis=1), axis=1)
    tracer = tracers
    for repeat in range(STEPS):
        ghost_rows = jnp.stack([tracer[:, :, -1], tracer[:, :, -2]], axis=2)
        whole_rows = lax.all_gather(ghost_rows, "lon", axis=3, tiled=True)
        ghost_rows = jnp.take(whole_rows, fold_partner, axis=3)
        extended = extended_2(tracer, (("lat", 2),), 2, False)
        top_rows = jnp.where(is_top, ghost_rows, extended[:, :, -2:])
        extended = jnp.concatenate([extended[:, :, :-2], top_rows], axis=2)
        extended = extended_2(extended, (("lon", 3),), 2, True)
        tracer = advance(extended, wet_mask, east_ext, north_ext, surface)
    return tracer


def solution(mesh):
    return jax.shard_map(
        per_device,
        mesh=mesh,
        in_specs=(
            P(None, None, "lat", "lon"),
            P(None, "lat", "lon"),
            P(None, "lat", "lon"),
            P("lat", "lon"),
            P("lon"),
            P(None, ("lon", "lat")),
            P(None, "lat", "lon"),
            P(None, "lat", "lon"),
        ),
        out_specs=P(None, None, "lat", "lon"),
        check_vma=False,
    )
```

profile of v0, /device:TPU:1, one launch (start us, length us, event | category | flops | bytes accessed | tf_op | source)
XLA Modules:
  0.0 800.2 jit_solution(17099343849323046629)
XLA Ops:
  3.0 3.3 collective-permute-start.5
  6.3 5.5 collective-permute-start.4
  16.2 5.1 collective-permute-start
  26.8 43.8 %all_gather.12 = f32[2,16,2,2048]{1,2,3,0:T(2,128)} all-gather(f32[2,16,2,256]{1,2,3,0:T(2,128)S(1)} %copy.114), channel_id=1, replica_groups=mesh['lon'=8,'lat'=16] {'lon'}, dimensions={3}, use_global_device_ids=true | all-gather | bytes 589824 | tf_op jit(solution)/shard_map/all_gather | solution.py:117
  70.6 3.5 gather_fusion.1
  74.6 448.2 %all_gather.13 = f32[2,65536]{0,1:T(8,128)} all-gather(f32[2,512]{0,1:T(8,128)S(1)} %copy.125), channel_id=1, replica_groups=mesh['lon'=8,'lat'=16] {'lon','lat'}, dimensions={1}, use_global_device_ids=true | all-gather | bytes 528384 | tf_op jit(solution)/shard_map/all_gather | solution.py:112
  522.9 65.2 %gather_fusion = f32[16384,2]{1,0:T(8,128)} fusion(f32[2,65536]{0,1:T(8,128)} %all_gather.13, s32[16384]{0:T(1024)S(1)} %broadcast_clamp_fusion), kind=kCustom, calls=%fused_computation.3 | custom fusion | bytes 327680 | tf_op jit(solution)/shard_map/jit(_take)/gather | solution.py:113
  588.1 7.0 multiply_reduce_fusion
  596.8 39.5 %collective-permute-start.7 = (f32[2,16,20,2]{3,1,2,0:T(8,128)S(1)}, f32[2,16,20,2]{3,1,2,0:T(8,128)S(1)}, u32[]{:S(2)}, u32[]{:S(2)}) collective-permute-start(f32[2,16,20,2]{3,1,2,0:T(8,128)S(1)} %get-tuple-element.25), channel_id=1, source_target_pairs={{16,0},{32,16},{48,32},{64,48},{80,64},{96,80},{112,96},{0,112},{1... | collective-permute-start | bytes 15368 | tf_op jit(solution)/shard_map/ppermute | solution.py:19
  637.6 3.6 collective-permute-start.3
  643.3 4.6 collective-permute-done.6
  648.3 4.3 collective-permute-done.3
  652.6 4.0 collective-permute-done.2
  667.1 25.3 %all_gather.14 = f32[2,16,2,2048]{3,1,2,0:T(8,128)} all-gather(f32[2,16,2,256]{3,1,2,0:T(8,128)S(1)} %pad_maximum_fusion.40), channel_id=1, replica_groups=mesh['lon'=8,'lat'=16] {'lon'}, dimensions={3}, use_global_device_ids=true | all-gather | bytes 589824 | tf_op jit(solution)/shard_map/all_gather | solution.py:117
  692.4 6.0 copy.129
  698.5 4.3 gather_fusion.2
  703.9 9.6 %collective-permute-start.8 = (f32[2,16,2,256]{3,1,2,0:T(8,128)S(1)}, f32[2,16,2,256]{3,1,2,0:T(8,128)S(1)}, u32[]{:S(2)}, u32[]{:S(2)}) collective-permute-start(f32[2,16,2,256]{3,1,2,0:T(8,128)S(1)} %get-tuple-element.36), channel_id=1, source_target_pairs={{0,1},{1,2},{2,3},{3,4},{4,5},{5,6},{6,7},{7,8},{8,9},{9,10},{10,1... | collective-permute-start | bytes 196616 | tf_op jit(solution)/shard_map/ppermute | solution.py:17
  713.6 6.7 collective-permute-done.8
  722.1 4.4 collective-permute-done.11
  735.4 25.0 %all_gather.15 = f32[2,16,2,2048]{3,1,2,0:T(8,128)} all-gather(f32[2,16,2,256]{3,1,2,0:T(8,128)S(1)} %pad_maximum_fusion.41), channel_id=1, replica_groups=mesh['lon'=8,'lat'=16] {'lon'}, dimensions={3}, use_global_device_ids=true | all-gather | bytes 589824 | tf_op jit(solution)/shard_map/all_gather | solution.py:117
  760.4 6.0 copy.131
  766.4 4.3 gather_fusion.3
  771.9 13.2 %collective-permute-start.12 = (f32[2,16,2,256]{3,1,2,0:T(8,128)}, f32[2,16,2,256]{3,1,2,0:T(8,128)S(1)}, u32[]{:S(2)}, u32[]{:S(2)}) collective-permute-start(f32[2,16,2,256]{3,1,2,0:T(8,128)} %get-tuple-element.32), channel_id=1, source_target_pairs={{0,1},{1,2},{2,3},{3,4},{4,5},{5,6},{6,7},{7,8},{8,9},{9,10},{10,1... | collective-permute-start | bytes 196616 | tf_op jit(solution)/shard_map/ppermute | solution.py:17
  788.6 4.4 collective-permute-done.15
  (138 shorter events, 52.6 us)
Async XLA Ops:
  3.0 592.8 %collective-permute-start.5 = (f32[2,16,2,256]{3,1,2,0:T(8,128)}, f32[2,16,2,256]{3,1,2,0:T(8,128)}, u32[]{:S(2)}, u32[]{:S(2)}) collective-permute-start(f32[2,16,2,256]{3,1,2,0:T(8,128)} %get-tuple-element.41), channel_id=1, source_target_pairs={{1,0},{2,1},{3,2},{4,3},{5,4},{6,5},{7,6},{8,7},{9,8},{10,9},{11,1... | collective-permute-start | bytes 196616 | tf_op jit(solution)/shard_map/ppermute | solution.py:19
  6.3 590.3 %collective-permute-start.4 = (f32[2,16,2,256]{3,1,2,0:T(8,128)}, f32[2,16,2,256]{3,1,2,0:T(8,128)S(1)}, u32[]{:S(2)}, u32[]{:S(2)}) collective-permute-start(f32[2,16,2,256]{3,1,2,0:T(8,128)} %get-tuple-element.40), channel_id=1, source_target_pairs={{0,1},{1,2},{2,3},{3,4},{4,5},{5,6},{6,7},{7,8},{8,9},{9,10},{10,1... | collective-permute-start | bytes 196616 | tf_op jit(solution)/shard_map/ppermute | solution.py:17
  12.6 61.8 %copy-start.15 = (f32[2,512]{1,0:T(2,128)S(1)}, f32[2,512]{1,0:T(2,128)}, u32[]{:S(2)}) copy-start(f32[2,512]{1,0:T(2,128)} %param.17) | copy-start | bytes 12292
  14.3 622.0 %collective-permute-start.1 = (f32[33,2,256]{2,1,0:T(2,128)}, f32[33,2,256]{2,1,0:T(2,128)}, u32[]{:S(2)}, u32[]{:S(2)}) collective-permute-start(f32[33,2,256]{2,1,0:T(2,128)} %get-tuple-element.31), channel_id=1, source_target_pairs={{1,0},{2,1},{3,2},{4,3},{5,4},{6,5},{7,6},{8,7},{9,8},{10,9},{11,1... | collective-permute-start | bytes 202760 | tf_op jit(solution)/shard_map/ppermute | solution.py:19
  16.2 621.0 %collective-permute-start = (f32[33,2,256]{2,1,0:T(2,128)}, f32[33,2,256]{2,1,0:T(2,128)S(1)}, u32[]{:S(2)}, u32[]{:S(2)}) collective-permute-start(f32[33,2,256]{2,1,0:T(2,128)} %get-tuple-element.30), channel_id=1, source_target_pairs={{0,1},{1,2},{2,3},{3,4},{4,5},{5,6},{6,7},{7,8},{8,9},{9,10},{10,1... | collective-permute-start | bytes 202760 | tf_op jit(solution)/shard_map/ppermute | solution.py:17
  74.6 513.5 %copy-start.14 = (f32[4,16,256]{2,1,0:T(8,128)S(1)}, f32[4,16,256]{2,1,0:T(8,128)}, u32[]{:S(2)}) copy-start(f32[4,16,256]{2,1,0:T(8,128)} %param.19) | copy-start | bytes 196612
  595.1 41.2 %copy-start.13 = (f32[33,2,256]{2,1,0:T(2,128)S(1)}, f32[33,2,256]{2,1,0:T(2,128)}, u32[]{:S(2)}) copy-start(f32[33,2,256]{2,1,0:T(2,128)} %constant.69.clone.1) | copy-start | bytes 202756
  595.1 42.2 %copy-start.4 = (f32[16,16,256]{2,1,0:T(8,128)S(1)}, f32[16,16,256]{2,1,0:T(8,128)}, u32[]{:S(2)}) copy-start(f32[16,16,256]{2,1,0:T(8,128)} %param.13) | copy-start | bytes 786436
  596.8 46.5 %collective-permute-start.7 = (f32[2,16,20,2]{3,1,2,0:T(8,128)S(1)}, f32[2,16,20,2]{3,1,2,0:T(8,128)S(1)}, u32[]{:S(2)}, u32[]{:S(2)}) collective-permute-start(f32[2,16,20,2]{3,1,2,0:T(8,128)S(1)} %get-tuple-element.25), channel_id=1, source_target_pairs={{16,0},{32,16},{48,32},{64,48},{80,64},{96,80},{112,96},{0,112},{1... | collective-permute-start | bytes 15368 | tf_op jit(solution)/shard_map/ppermute | solution.py:19
  636.3 11.6 %collective-permute-start.6 = (f32[2,16,20,2]{3,1,2,0:T(8,128)S(1)}, f32[2,16,20,2]{3,1,2,0:T(8,128)S(1)}, u32[]{:S(2)}, u32[]{:S(2)}) collective-permute-start(f32[2,16,20,2]{3,1,2,0:T(8,128)S(1)} %get-tuple-element.24), channel_id=1, source_target_pairs={{0,16},{16,32},{32,48},{48,64},{64,80},{80,96},{96,112},{112,0},{1... | collective-permute-start | bytes 15368 | tf_op jit(solution)/shard_map/ppermute | solution.py:17
  637.6 15.0 %collective-permute-start.3 = (f32[33,20,2]{2,1,0:T(8,128)S(1)}, f32[33,20,2]{2,1,0:T(8,128)S(1)}, u32[]{:S(2)}, u32[]{:S(2)}) collective-permute-start(f32[33,20,2]{2,1,0:T(8,128)S(1)} %get-tuple-element.19), channel_id=1, source_target_pairs={{16,0},{32,16},{48,32},{64,48},{80,64},{96,80},{112,96},{0,112},{1... | collective-permute-start | bytes 15848 | tf_op jit(solution)/shard_map/ppermute | solution.py:19
  641.2 15.4 %collective-permute-start.2 = (f32[33,20,2]{2,1,0:T(8,128)S(1)}, f32[33,20,2]{2,1,0:T(8,128)S(1)}, u32[]{:S(2)}, u32[]{:S(2)}) collective-permute-start(f32[33,20,2]{2,1,0:T(8,128)S(1)} %get-tuple-element.18), channel_id=1, source_target_pairs={{0,16},{16,32},{32,48},{48,64},{64,80},{80,96},{96,112},{112,0},{1... | collective-permute-start | bytes 15848 | tf_op jit(solution)/shard_map/ppermute | solution.py:17
  658.9 2.3 copy-start.1
  660.1 2.3 copy-start.6
  663.8 49.7 %collective-permute-start.9 = (f32[2,16,2,256]{3,1,2,0:T(8,128)S(1)}, f32[2,16,2,256]{3,1,2,0:T(8,128)S(1)}, u32[]{:S(2)}, u32[]{:S(2)}) collective-permute-start(f32[2,16,2,256]{3,1,2,0:T(8,128)S(1)} %get-tuple-element.37), channel_id=1, source_target_pairs={{1,0},{2,1},{3,2},{4,3},{5,4},{6,5},{7,6},{8,7},{9,8},{10,9},{11,1... | collective-permute-start | bytes 196616 | tf_op jit(solution)/shard_map/ppermute | solution.py:19
  692.4 29.6 %copy-start.10 = (f32[15,16,256]{2,0,1:T(8,128)S(1)}, f32[15,16,256]{2,0,1:T(8,128)}, u32[]{:S(2)}) copy-start(f32[15,16,256]{2,0,1:T(8,128)} %copy-done.9) | copy-start | bytes 737284
  703.9 16.3 %collective-permute-start.8 = (f32[2,16,2,256]{3,1,2,0:T(8,128)S(1)}, f32[2,16,2,256]{3,1,2,0:T(8,128)S(1)}, u32[]{:S(2)}, u32[]{:S(2)}) collective-permute-start(f32[2,16,2,256]{3,1,2,0:T(8,128)S(1)} %get-tuple-element.36), channel_id=1, source_target_pairs={{0,1},{1,2},{2,3},{3,4},{4,5},{5,6},{6,7},{7,8},{8,9},{9,10},{10,1... | collective-permute-start | bytes 196616 | tf_op jit(solution)/shard_map/ppermute | solution.py:17
  720.5 6.0 collective-permute-start.11
  720.5 8.3 %collective-permute-start.10 = (f32[2,16,20,2]{3,1,2,0:T(8,128)S(1)}, f32[2,16,20,2]{3,1,2,0:T(8,128)S(1)}, u32[]{:S(2)}, u32[]{:S(2)}) collective-permute-start(f32[2,16,20,2]{3,1,2,0:T(8,128)S(1)} %get-tuple-element.22), channel_id=1, source_target_pairs={{0,16},{16,32},{32,48},{48,64},{64,80},{80,96},{96,112},{112,0},{1... | collective-permute-start | bytes 15368 | tf_op jit(solution)/shard_map/ppermute | solution.py:17
  733.5 51.7 %collective-permute-start.13 = (f32[2,16,2,256]{3,1,2,0:T(8,128)S(1)}, f32[2,16,2,256]{3,1,2,0:T(8,128)S(1)}, u32[]{:S(2)}, u32[]{:S(2)}) collective-permute-start(f32[2,16,2,256]{3,1,2,0:T(8,128)S(1)} %get-tuple-element.33), channel_id=1, source_target_pairs={{1,0},{2,1},{3,2},{4,3},{5,4},{6,5},{7,6},{8,7},{9,8},{10,9},{11,1... | collective-permute-start | bytes 196616 | tf_op jit(solution)/shard_map/ppermute | solution.py:19
  760.4 28.1 %copy-start.11 = (f32[15,16,256]{2,0,1:T(8,128)S(1)}, f32[15,16,256]{2,0,1:T(8,128)}, u32[]{:S(2)}) copy-start(f32[15,16,256]{2,0,1:T(8,128)} %copy-done.9) | copy-start | bytes 737284
  771.9 14.8 %collective-permute-start.12 = (f32[2,16,2,256]{3,1,2,0:T(8,128)}, f32[2,16,2,256]{3,1,2,0:T(8,128)S(1)}, u32[]{:S(2)}, u32[]{:S(2)}) collective-permute-start(f32[2,16,2,256]{3,1,2,0:T(8,128)} %get-tuple-element.32), channel_id=1, source_target_pairs={{0,1},{1,2},{2,3},{3,4},{4,5},{5,6},{6,7},{7,8},{8,9},{9,10},{10,1... | collective-permute-start | bytes 196616 | tf_op jit(solution)/shard_map/ppermute | solution.py:17
  787.0 6.0 collective-permute-start.15
  787.1 8.1 %collective-permute-start.14 = (f32[2,16,20,2]{3,1,2,0:T(8,128)S(1)}, f32[2,16,20,2]{3,1,2,0:T(8,128)S(1)}, u32[]{:S(2)}, u32[]{:S(2)}) collective-permute-start(f32[2,16,20,2]{3,1,2,0:T(8,128)S(1)} %get-tuple-element.20), channel_id=1, source_target_pairs={{0,16},{16,32},{32,48},{48,64},{64,80},{80,96},{96,112},{112,0},{1... | collective-permute-start | bytes 15368 | tf_op jit(solution)/shard_map/ppermute | solution.py:17
  (8 other events, 9.1 us)
where the time goes:
time: 802 us; the launch traced here: 800 us
  blocking collectives  542 us (68%)
  local copies, waits for them, and re-layouts  100 us (12%)
  starting transfers between devices  90 us (11%)
  waiting for transfers between devices  36.6 us (5%)
  other arithmetic  30.6 us (4%)
    all_gather x1, blocking collectives, per_device(): gathered = lax.all_gather(atm_flux, ('lon', 'lat'), axis=1, tiled=True)  448 us
    all_gather x3, blocking collectives, per_device(): whole_rows = lax.all_gather(ghost_rows, 'lon', axis=3, tiled=True)  94.2 us
    gather x1, local copies, waits for them, and re-layouts, per_device(): jnp.take(gathered, remap_index, axis=1)  65.2 us
    ppermute x8, starting transfers between devices, extended_2(): lax.ppermute(head, axis, [((i + 1) % count, i) for i in range(ends)])  53.6 us
    ppermute x8, starting transfers between devices, extended_2(): lax.ppermute(tail, axis, [(i, (i + 1) % count) for i in range(ends)])  36.3 us
    ppermute x8, waiting for transfers between devices, extended_2(): lax.ppermute(tail, axis, [(i, (i + 1) % count) for i in range(ends)])  21.5 us
  transfers between devices with their start and end apart: 16, of which 10 were waited for; matrix products, arithmetic and copies ran while one was open for 14% of the time, Pallas kernels for 0%

commit v1 on v0

--- a/solution.py
+++ b/solution.py
@@ -114,7 +114,9 @@
     tracer = tracers
     for repeat in range(STEPS):
         ghost_rows = jnp.stack([tracer[:, :, -1], tracer[:, :, -2]], axis=2)
-        whole_rows = lax.all_gather(ghost_rows, "lon", axis=3, tiled=True)
+        whole_rows = jnp.concatenate(
+            lax.all_to_all(jnp.stack([ghost_rows] * lax.axis_size("lon")), "lon", 0, 0), axis=3
+        )
         ghost_rows = jnp.take(whole_rows, fold_partner, axis=3)
         extended = extended_2(tracer, (("lat", 2),), 2, False)
         top_rows = jnp.where(is_top, ghost_rows, extended[:, :, -2:])

time: 802 us -> 729 us (0.909)
  blocking collectives: 542 us -> 462 us
  starting transfers between devices: 90 us -> 53.8 us
  waiting for transfers between devices: 36.6 us -> 67.6 us
    all_gather x3 -> x0, blocking collectives: 94.2 us -> none  [per_device(): whole_rows = lax.all_gather(ghost_rows, 'lon', axis=3, tiled=True)]
    ppermute x8, starting transfers between devices: 53.6 us -> 18.6 us  [extended_2(): lax.ppermute(head, axis, [((i + 1) % count, i) for i in range(ends)])]
    ppermute x8, waiting for transfers between devices: 21.5 us -> 39.5 us  [extended_2(): lax.ppermute(tail, axis, [(i, (i + 1) % count) for i in range(ends)])]
    reshape x0 -> x3, local copies, waits for them, and re-layouts: none -> 14.7 us  [per_device(): jnp.concatenate(lax.all_to_all(jnp.stack([ghost_rows] * lax.axis_size('lo...]
    all_gather x1, blocking collectives: 448 us -> 462 us  [per_device(): gathered = lax.all_gather(atm_flux, ('lon', 'lat'), axis=1, tiled=True)]
    ppermute x8, starting transfers between devices: 36.3 us -> 22.7 us  [extended_2(): lax.ppermute(tail, axis, [(i, (i + 1) % count) for i in range(ends)])]
    all_to_all x0 -> x3, starting transfers between devices: none -> 12.5 us  [per_device(): lax.all_to_all(jnp.stack([ghost_rows] * lax.axis_size('lon')), 'lon', 0, 0)]
    all_gather x2 -> x0, local copies, waits for them, and re-layouts: 12 us -> none  [per_device(): whole_rows = lax.all_gather(ghost_rows, 'lon', axis=3, tiled=True)]
  transfers between devices with their start and end apart: 16 -> 19, of which waited for: 10 -> 9; matrix products, arithmetic and copies ran while one was open for 14% -> 17% of each run, Pallas kernels for 0% -> 0%
where the time goes in v1:
time: 729 us; the launch traced here: 727 us
  blocking collectives  462 us (63%)
  local copies, waits for them, and re-layouts  105 us (14%)
  waiting for transfers between devices  67.6 us (9%)
  starting transfers between devices  53.8 us (7%)
  other arithmetic  38.1 us (5%)
    all_gather x1, blocking collectives, per_device(): gathered = lax.all_gather(atm_flux, ('lon', 'lat'), axis=1, tiled=True)  462 us
    gather x1, local copies, waits for them, and re-layouts, per_device(): jnp.take(gathered, remap_index, axis=1)  65.3 us
    ppermute x8, waiting for transfers between devices, extended_2(): lax.ppermute(tail, axis, [(i, (i + 1) % count) for i in range(ends)])  39.5 us
    ppermute x8, waiting for transfers between devices, extended_2(): lax.ppermute(head, axis, [((i + 1) % count, i) for i in range(ends)])  25.9 us
    ppermute x8, starting transfers between devices, extended_2(): lax.ppermute(tail, axis, [(i, (i + 1) % count) for i in range(ends)])  22.7 us
    ppermute x8, starting transfers between devices, extended_2(): lax.ppermute(head, axis, [((i + 1) % count, i) for i in range(ends)])  18.6 us
    reshape x3, local copies, waits for them, and re-layouts, per_device(): jnp.concatenate(lax.all_to_all(jnp.stack([ghost_rows] * lax.axis_size('lo...  14.7 us
  transfers between devices with their start and end apart: 19, of which 9 were waited for; matrix products, arithmetic and copies ran while one was open for 17% of the time, Pallas kernels for 0%

profile of v1, /device:TPU:1, one launch (start us, length us, event | category | flops | bytes accessed | tf_op | source)
XLA Modules:
  0.0 727.2 jit_solution(3678754326948746753)
XLA Ops:
  3.0 3.3 collective-permute-start.5
  7.2 5.5 all-to-all-start
  12.7 5.4 collective-permute-start.4
  22.5 5.1 collective-permute-start
  29.9 462.0 %all_gather.3 = f32[2,65536]{0,1:T(8,128)} all-gather(f32[2,512]{0,1:T(8,128)S(1)} %copy.133), channel_id=1, replica_groups=mesh['lon'=8,'lat'=16] {'lon','lat'}, dimensions={1}, use_global_device_ids=true | all-gather | bytes 528384 | tf_op jit(solution)/shard_map/all_gather | solution.py:112
  492.0 65.3 %gather_fusion = f32[16384,2]{1,0:T(8,128)} fusion(f32[2,65536]{0,1:T(8,128)} %all_gather.3, s32[16384]{0:T(1024)S(1)} %broadcast_clamp_fusion), kind=kCustom, calls=%fused_computation.3 | custom fusion | bytes 327680 | tf_op jit(solution)/shard_map/jit(_take)/gather | solution.py:113
  557.2 7.2 multiply_reduce_fusion
  569.8 8.0 %collective-permute-done.3 = f32[33,20,2]{2,1,0:T(8,128)} collective-permute-done((f32[33,20,2]{2,1,0:T(8,128)}, f32[33,20,2]{2,1,0:T(8,128)}, u32[]{:S(2)}, u32[]{:S(2)}) %collective-permute-start.3) | collective-permute-done | bytes 5312 | tf_op jit(solution)/shard_map/ppermute | solution.py:19
  577.8 29.4 %collective-permute-done.2 = f32[33,20,2]{2,1,0:T(8,128)} collective-permute-done((f32[33,20,2]{2,1,0:T(8,128)}, f32[33,20,2]{2,1,0:T(8,128)}, u32[]{:S(2)}, u32[]{:S(2)}) %collective-permute-start.2) | collective-permute-done | bytes 5312 | tf_op jit(solution)/shard_map/ppermute | solution.py:17
  614.7 6.1 copy.144
  620.7 4.3 gather_fusion.1
  632.2 4.5 collective-permute-done.7
  645.7 3.5 all-to-all-start.1
  649.3 4.5 collective-permute-start.9
  653.8 5.9 collective-permute-start.8
  659.7 4.3 copy.147
  664.0 3.6 gather_fusion.2
  671.5 6.5 collective-permute-done.11
  678.0 4.3 collective-permute-done.10
  687.4 3.5 all-to-all-start.2
  693.5 5.4 collective-permute-start.12
  701.1 4.3 copy.148
  705.4 3.5 gather_fusion.3
  712.0 7.0 collective-permute-done.15
  (192 shorter events, 64.0 us)
Async XLA Ops:
  0.0 29.8 %copy-start.37 = (f32[2,512]{1,0:T(2,128)S(1)}, f32[2,512]{1,0:T(2,128)}, u32[]{:S(2)}) copy-start(f32[2,512]{1,0:T(2,128)} %param.17) | copy-start | bytes 12292
  3.0 623.2 %collective-permute-start.5 = (f32[2,16,2,256]{3,1,2,0:T(8,128)}, f32[2,16,2,256]{3,1,2,0:T(8,128)}, u32[]{:S(2)}, u32[]{:S(2)}) collective-permute-start(f32[2,16,2,256]{3,1,2,0:T(8,128)} %get-tuple-element.41), channel_id=1, source_target_pairs={{1,0},{2,1},{3,2},{4,3},{5,4},{6,5},{7,6},{8,7},{9,8},{10,9},{11,1... | collective-permute-start | bytes 196616 | tf_op jit(solution)/shard_map/ppermute | solution.py:19
  7.2 607.4 %all-to-all-start = ((f32[8,2,16,2,256]{4,2,3,1,0:T(8,128)}), f32[8,2,16,2,256]{4,2,3,1,0:T(8,128)}, u32[]{:S(2)}, u32[]{:S(2)}) async-start(f32[8,2,16,2,256]{4,2,3,1,0:T(8,128)} %stack.13), calls=%async_computation | async-start | bytes 1048576 | tf_op jit(solution)/shard_map/all_to_all | solution.py:118
  12.7 614.5 %collective-permute-start.4 = (f32[2,16,2,256]{3,1,2,0:T(8,128)}, f32[2,16,2,256]{3,1,2,0:T(8,128)}, u32[]{:S(2)}, u32[]{:S(2)}) collective-permute-start(f32[2,16,2,256]{3,1,2,0:T(8,128)} %get-tuple-element.40), channel_id=1, source_target_pairs={{0,1},{1,2},{2,3},{3,4},{4,5},{5,6},{6,7},{7,8},{8,9},{9,10},{10,1... | collective-permute-start | bytes 196616 | tf_op jit(solution)/shard_map/ppermute | solution.py:17
  20.6 543.9 %collective-permute-start.1 = (f32[33,2,256]{2,1,0:T(2,128)S(1)}, f32[33,2,256]{2,1,0:T(2,128)}, u32[]{:S(2)}, u32[]{:S(2)}) collective-permute-start(f32[33,2,256]{2,1,0:T(2,128)S(1)} %get-tuple-element.31), channel_id=1, source_target_pairs={{1,0},{2,1},{3,2},{4,3},{5,4},{6,5},{7,6},{8,7},{9,8},{10,9},{11,1... | collective-permute-start | bytes 202760 | tf_op jit(solution)/shard_map/ppermute | solution.py:19
  22.5 542.9 %collective-permute-start = (f32[33,2,256]{2,1,0:T(2,128)}, f32[33,2,256]{2,1,0:T(2,128)S(1)}, u32[]{:S(2)}, u32[]{:S(2)}) collective-permute-start(f32[33,2,256]{2,1,0:T(2,128)} %get-tuple-element.30), channel_id=1, source_target_pairs={{0,1},{1,2},{2,3},{3,4},{4,5},{5,6},{6,7},{7,8},{8,9},{9,10},{10,1... | collective-permute-start | bytes 202760 | tf_op jit(solution)/shard_map/ppermute | solution.py:17
  28.3 598.0 %copy-start.35 = (pred[256]{0:T(512)(128)(4,1)}, pred[256]{0:T(512)(128)(4,1)S(1)}, u32[]{:S(2)}) copy-start(pred[256]{0:T(512)(128)(4,1)S(1)} %compare_and_fusion.1) | copy-start | bytes 772
  564.5 56.2 %copy-start.33 = (s32[1024]{0:T(1024)}, s32[1024]{0:T(1024)S(1)}, u32[]{:S(2)}) copy-start(s32[1024]{0:T(1024)S(1)} %pad_clamp_fusion) | copy-start | bytes 12292
  566.6 11.2 %collective-permute-start.3 = (f32[33,20,2]{2,1,0:T(8,128)}, f32[33,20,2]{2,1,0:T(8,128)}, u32[]{:S(2)}, u32[]{:S(2)}) collective-permute-start(f32[33,20,2]{2,1,0:T(8,128)} %get-tuple-element.19), channel_id=1, source_target_pairs={{16,0},{32,16},{48,32},{64,48},{80,64},{96,80},{112,96},{0,112},{1... | collective-permute-start | bytes 15848 | tf_op jit(solution)/shard_map/ppermute | solution.py:19
  567.7 39.4 %collective-permute-start.2 = (f32[33,20,2]{2,1,0:T(8,128)}, f32[33,20,2]{2,1,0:T(8,128)}, u32[]{:S(2)}, u32[]{:S(2)}) collective-permute-start(f32[33,20,2]{2,1,0:T(8,128)} %get-tuple-element.18), channel_id=1, source_target_pairs={{0,16},{16,32},{32,48},{48,64},{64,80},{80,96},{96,112},{112,0},{1... | collective-permute-start | bytes 15848 | tf_op jit(solution)/shard_map/ppermute | solution.py:17
  569.8 39.2 %copy-start.14 = (f32[16,16,256]{2,1,0:T(8,128)S(1)}, f32[16,16,256]{2,1,0:T(8,128)}, u32[]{:S(2)}) copy-start(f32[16,16,256]{2,1,0:T(8,128)} %param.13) | copy-start | bytes 786436
  569.8 39.2 %copy-start.23 = (f32[1,16,256]{2,1,0:T(8,128)S(1)}, f32[1,16,256]{2,1,0:T(8,128)}, u32[]{:S(2)}) copy-start(f32[1,16,256]{2,1,0:T(8,128)} %copy-done.21) | copy-start | bytes 49156
  628.3 8.3 %collective-permute-start.7 = (f32[2,16,20,2]{3,1,2,0:T(8,128)S(1)}, f32[2,16,20,2]{3,1,2,0:T(8,128)S(1)}, u32[]{:S(2)}, u32[]{:S(2)}) collective-permute-start(f32[2,16,20,2]{3,1,2,0:T(8,128)S(1)} %get-tuple-element.25), channel_id=1, source_target_pairs={{16,0},{32,16},{48,32},{64,48},{80,64},{96,80},{112,96},{0,112},{1... | collective-permute-start | bytes 15368 | tf_op jit(solution)/shard_map/ppermute | solution.py:19
  629.5 9.8 %collective-permute-start.6 = (f32[2,16,20,2]{3,1,2,0:T(8,128)S(1)}, f32[2,16,20,2]{3,1,2,0:T(8,128)S(1)}, u32[]{:S(2)}, u32[]{:S(2)}) collective-permute-start(f32[2,16,20,2]{3,1,2,0:T(8,128)S(1)} %get-tuple-element.24), channel_id=1, source_target_pairs={{0,16},{16,32},{32,48},{48,64},{64,80},{80,96},{96,112},{112,0},{1... | collective-permute-start | bytes 15368 | tf_op jit(solution)/shard_map/ppermute | solution.py:17
  645.7 14.0 %all-to-all-start.1 = ((f32[8,2,16,2,256]{4,2,3,1,0:T(8,128)}), f32[8,2,16,2,256]{4,2,3,1,0:T(8,128)S(1)}, u32[]{:S(2)}, u32[]{:S(2)}) async-start(f32[8,2,16,2,256]{4,2,3,1,0:T(8,128)} %stack.15), calls=%async_computation.1 | async-start | bytes 1048576 | tf_op jit(solution)/shard_map/all_to_all | solution.py:118
  649.3 18.6 %collective-permute-start.9 = (f32[2,16,2,256]{3,1,2,0:T(8,128)S(1)}, f32[2,16,2,256]{3,1,2,0:T(8,128)S(1)}, u32[]{:S(2)}, u32[]{:S(2)}) collective-permute-start(f32[2,16,2,256]{3,1,2,0:T(8,128)S(1)} %get-tuple-element.37), channel_id=1, source_target_pairs={{1,0},{2,1},{3,2},{4,3},{5,4},{6,5},{7,6},{8,7},{9,8},{10,9},{11,1... | collective-permute-start | bytes 196616 | tf_op jit(solution)/shard_map/ppermute | solution.py:19
  653.8 14.1 %collective-permute-start.8 = (f32[2,16,2,256]{3,1,2,0:T(8,128)S(1)}, f32[2,16,2,256]{3,1,2,0:T(8,128)S(1)}, u32[]{:S(2)}, u32[]{:S(2)}) collective-permute-start(f32[2,16,2,256]{3,1,2,0:T(8,128)S(1)} %get-tuple-element.36), channel_id=1, source_target_pairs={{0,1},{1,2},{2,3},{3,4},{4,5},{5,6},{6,7},{7,8},{8,9},{9,10},{10,1... | collective-permute-start | bytes 196616 | tf_op jit(solution)/shard_map/ppermute | solution.py:17
  668.2 9.8 %collective-permute-start.11 = (f32[2,16,20,2]{3,1,2,0:T(8,128)S(1)}, f32[2,16,20,2]{3,1,2,0:T(8,128)S(1)}, u32[]{:S(2)}, u32[]{:S(2)}) collective-permute-start(f32[2,16,20,2]{3,1,2,0:T(8,128)S(1)} %get-tuple-element.23), channel_id=1, source_target_pairs={{16,0},{32,16},{48,32},{64,48},{80,64},{96,80},{112,96},{0,112},{1... | collective-permute-start | bytes 15368 | tf_op jit(solution)/shard_map/ppermute | solution.py:19
  671.4 10.9 %collective-permute-start.10 = (f32[2,16,20,2]{3,1,2,0:T(8,128)S(1)}, f32[2,16,20,2]{3,1,2,0:T(8,128)S(1)}, u32[]{:S(2)}, u32[]{:S(2)}) collective-permute-start(f32[2,16,20,2]{3,1,2,0:T(8,128)S(1)} %get-tuple-element.22), channel_id=1, source_target_pairs={{0,16},{16,32},{32,48},{48,64},{64,80},{80,96},{96,112},{112,0},{1... | collective-permute-start | bytes 15368 | tf_op jit(solution)/shard_map/ppermute | solution.py:17
  687.4 13.8 %all-to-all-start.2 = ((f32[8,2,16,2,256]{4,2,3,1,0:T(8,128)}), f32[8,2,16,2,256]{4,2,3,1,0:T(8,128)S(1)}, u32[]{:S(2)}, u32[]{:S(2)}) async-start(f32[8,2,16,2,256]{4,2,3,1,0:T(8,128)} %stack.17), calls=%async_computation.2 | async-start | bytes 1048576 | tf_op jit(solution)/shard_map/all_to_all | solution.py:118
  691.5 17.7 %collective-permute-start.13 = (f32[2,16,2,256]{3,1,2,0:T(8,128)}, f32[2,16,2,256]{3,1,2,0:T(8,128)}, u32[]{:S(2)}, u32[]{:S(2)}) collective-permute-start(f32[2,16,2,256]{3,1,2,0:T(8,128)} %get-tuple-element.33), channel_id=1, source_target_pairs={{1,0},{2,1},{3,2},{4,3},{5,4},{6,5},{7,6},{8,7},{9,8},{10,9},{11,1... | collective-permute-start | bytes 196616 | tf_op jit(solution)/shard_map/ppermute | solution.py:19
  693.5 16.6 %collective-permute-start.12 = (f32[2,16,2,256]{3,1,2,0:T(8,128)}, f32[2,16,2,256]{3,1,2,0:T(8,128)S(1)}, u32[]{:S(2)}, u32[]{:S(2)}) collective-permute-start(f32[2,16,2,256]{3,1,2,0:T(8,128)} %get-tuple-element.32), channel_id=1, source_target_pairs={{0,1},{1,2},{2,3},{3,4},{4,5},{5,6},{6,7},{7,8},{8,9},{9,10},{10,1... | collective-permute-start | bytes 196616 | tf_op jit(solution)/shard_map/ppermute | solution.py:17
  710.3 8.6 %collective-permute-start.15 = (f32[2,16,20,2]{3,1,2,0:T(8,128)S(1)}, f32[2,16,20,2]{3,1,2,0:T(8,128)S(1)}, u32[]{:S(2)}, u32[]{:S(2)}) collective-permute-start(f32[2,16,20,2]{3,1,2,0:T(8,128)S(1)} %get-tuple-element.21), channel_id=1, source_target_pairs={{16,0},{32,16},{48,32},{64,48},{80,64},{96,80},{112,96},{0,112},{1... | collective-permute-start | bytes 15368 | tf_op jit(solution)/shard_map/ppermute | solution.py:19
  711.7 10.4 %collective-permute-start.14 = (f32[2,16,20,2]{3,1,2,0:T(8,128)S(1)}, f32[2,16,20,2]{3,1,2,0:T(8,128)S(1)}, u32[]{:S(2)}, u32[]{:S(2)}) collective-permute-start(f32[2,16,20,2]{3,1,2,0:T(8,128)S(1)} %get-tuple-element.20), channel_id=1, source_target_pairs={{0,16},{16,32},{32,48},{48,64},{64,80},{80,96},{96,112},{112,0},{1... | collective-permute-start | bytes 15368 | tf_op jit(solution)/shard_map/ppermute | solution.py:17
  (35 other events, 335.1 us)
